TPU v7x, 256 devices: a whole 4x4x8 slice. The times are simulated.
256 devices in a mesh: cell: 64 (over y, z, core), spot: 4 (over x).
Axes of the slice: x: 4, y: 4, z: 8, core: 2. Of those that a mesh axis runs over, the one named last changes fastest.
Arguments:
- cells_pca: float32 [50, 32768], P(None, 'cell'), may hold values from -8 to 8
- spots_pca: float32 [50, 32768], P(None, ('spot', 'cell')), may hold values from -8 to 8
- log_a: float32 [32768], P('cell'), may hold values from -1 to 1
- log_b: float32 [32768], P('spot'), may hold values from -1 to 1
Outputs:
- cell_potential: float32 [32768], P('cell')
- spot_potential: float32 [32768], P('spot')
- barycenter: float32 [50, 32768], P(None, 'cell')
All inputs are finite; a program needn't handle non-finite values.
Results may differ from a plain program's by a relative error of at most 0.0003.
Values sent between devices are 32-bit elements; how exact they have to be, the bound alone decides.
A program may use at most 128 MiB of HBM per device.

v0:
```python
import jax
import jax.numpy as jnp
from jax import lax
from jax.sharding import PartitionSpec as P

ITERS = 2


blur = 0.25


def row_lse(tile, spot_potential):
    scores = (spot_potential[None, :] - tile) / blur
    local_top = jnp.max(scores, axis=1)
    top = lax.pmax(local_top, "spot")
    total = lax.psum(jnp.sum(jnp.exp(scores - top[:, None]), axis=1), "spot")
    return top + jnp.log(total)


def col_lse(tile, cell_potential):
    scores = (cell_potential[:, None] - tile) / blur
    local_top = jnp.max(scores, axis=0)
    top = lax.pmax(local_top, "cell")
    total = lax.psum(jnp.sum(jnp.exp(scores - top[None, :]), axis=0), "cell")
    return top + jnp.log(total)


def on_device(cells_pca, spots_pca, log_a, log_b):
    spots = lax.all_gather(spots_pca, "cell", axis=1, tiled=True)
    cell_norm = jnp.sum(cells_pca * cells_pca, axis=0)
    spot_norm = jnp.sum(spots * spots, axis=0)
    cross = jnp.dot(
        cells_pca.T, spots, precision=lax.Precision.HIGHEST, preferred_element_type=jnp.float32
    )
    tile = cell_norm[:, None] + spot_norm[None, :] - 2.0 * cross
    spot_potential = jnp.zeros((spots.shape[1],), jnp.float32)
    cell_potential = jnp.zeros((cells_pca.shape[1],), jnp.float32)
    for step in range(ITERS):
        cell_potential = blur * log_a - blur * row_lse(tile, spot_potential)
        spot_potential = blur * log_b - blur * col_lse(tile, cell_potential)
    scores = (spot_potential[None, :] - tile) / blur
    local_top = jnp.max(scores, axis=1)
    top = lax.pmax(local_top, "spot")
    weight = jnp.exp(scores - top[:, None])
    numer = jnp.dot(
        spots, weight.T, precision=lax.Precision.HIGHEST, preferred_element_type=jnp.float32
    )
    numer, total = lax.psum((numer, jnp.sum(weight, axis=1)), "spot")
    barycenter = numer / total[None, :]
    return (cell_potential, spot_potential, barycenter)


def solution(mesh):
    placed = (P(None, "cell"), P(None, ("spot", "cell")), P("cell"), P("spot"))
    return jax.shard_map(
        on_device,
        mesh=mesh,
        in_specs=placed,
        out_specs=(P("cell"), P("spot"), P(None, "cell")),
        check_vma=False,
    )
```

profile of v0, /device:TPU:24, one launch (start us, length us, event | category | flops | bytes accessed | tf_op | source)
XLA Modules:
  0.0 1275.9 jit_solution(16703686660252518371)
XLA Ops:
  7.2 0.0 all-gather.2.cloned.1.call-start
  7.2 0.7 all-gather.2.cloned.1.call-update
  7.9 0.0 all-reduce.2.cloned.1.call-start
  7.9 0.9 multiply_reduce_fusion.1
  8.9 76.3 %all-gather.2.cloned.1.call-done = f32[50,8192]{1,0:T(8,128)} async-done(((f32[50,128]{1,0:T(8,128)}), f32[50,8192]{1,0:T(8,128)}) %all-gather.2.cloned.1.call-update) | async-done | bytes 1638416 | tf_op jit(solution)/shard_map/all_gather | solution.py:29
  85.2 1.7 multiply_reduce_fusion
  86.9 0.0 copy-start.4
  86.9 19.8 %fusion = (f32[512]{0:T(512)S(1)}, f32[512,8192]{1,0:T(8,128)}) fusion(f32[50,512]{1,0:T(8,128)} %param.4, f32[50,8192]{1,0:T(8,128)} %all-gather.2.cloned.1.call-done, f32[8192]{0:T(1024)S(1)} %multiply_reduce_fusion, f32[512]{0:T(512)S(1)} %multiply_reduce_fusion.1), kind=kOutput, calls=%fused_computation.11 | convolution fusion | flops 2541747712 | bytes 18554880 | tf_op jit(solution)/shard_map/dot_general | solution.py:32
  106.6 10.4 pmax.35
  117.0 9.1 exponential_reduce_fusion.3
  126.2 7.7 psum.42
  133.9 0.0 copy-done.4
  133.9 0.0 copy-start.2
  133.9 8.4 fusion.1
  142.3 210.9 %pmax.36 = f32[8192]{0:T(1024)S(1)} all-reduce(f32[8192]{0:T(1024)S(1)} %fusion.1), channel_id=1, replica_groups=mesh['cell'=64,'spot'=4] {'cell'}, use_global_device_ids=true, to_apply=%region_7.0 | all-reduce | flops 8192 | bytes 65536 | tf_op jit(solution)/shard_map/pmax | solution.py:23
  353.2 9.4 exponential_reduce_fusion.2
  362.6 246.1 %psum.43 = f32[8192]{0:T(1024)S(1)} all-reduce(f32[8192]{0:T(1024)S(1)} %exponential_reduce_fusion.2), channel_id=1, replica_groups=mesh['cell'=64,'spot'=4] {'cell'}, use_global_device_ids=true, to_apply=%region_9.0 | all-reduce | flops 8192 | bytes 65536 | tf_op jit(solution)/shard_map/psum | solution.py:24
  608.7 0.0 copy-done.2
  608.8 7.5 fusion.2
  616.3 9.8 pmax.37
  626.0 9.1 exponential_reduce_fusion.1
  635.2 7.9 psum.44
  643.1 0.0 copy-start.3
  643.1 8.3 fusion.3
  651.5 246.1 %pmax.38 = f32[8192]{0:T(1024)S(1)} all-reduce(f32[8192]{0:T(1024)S(1)} %fusion.3), channel_id=1, replica_groups=mesh['cell'=64,'spot'=4] {'cell'}, use_global_device_ids=true, to_apply=%region_15.0 | all-reduce | flops 8192 | bytes 65536 | tf_op jit(solution)/shard_map/pmax | solution.py:23
  897.6 0.0 copy-start
  897.6 9.5 exponential_reduce_fusion
  907.2 0.0 copy-done.3
  907.2 246.1 %psum.45 = f32[8192]{0:T(1024)S(1)} all-reduce(f32[8192]{0:T(1024)S(1)} %exponential_reduce_fusion), channel_id=1, replica_groups=mesh['cell'=64,'spot'=4] {'cell'}, use_global_device_ids=true, to_apply=%region_17.0 | all-reduce | flops 8192 | bytes 65536 | tf_op jit(solution)/shard_map/psum | solution.py:24
  1153.3 0.0 copy-start.1
  1153.3 7.5 fusion.4
  1160.9 10.0 pmax.39
  1170.8 0.0 copy-done
  1170.8 22.8 %fusion.10 = f32[50,512]{1,0:T(8,128)} fusion(f32[50,8192]{1,0:T(8,128)S(1)} %copy-done, f32[512,8192]{1,0:T(8,128)} %get-tuple-element.4, f32[512]{0:T(512)S(1)} %pmax.39, f32[8192]{0:T(1024)S(1)} %multiply_subtract_fusion.1), kind=kOutput, calls=%fused_computation.22 | convolution fusion | flops 2529165312 | bytes 18552832 | tf_op jit(solution)/shard_map/dot_general | solution.py:45
  1193.7 0.0 all-reduce.2.cloned.1.call-update
  1193.7 0.0 copy-done.1
  1193.7 9.1 fusion.5
  1202.8 7.7 psum.47
  1210.6 56.7 %all-reduce.2.cloned.1.call-done = f32[50,512]{1,0:T(8,128)} async-done(((f32[50,512]{1,0:T(8,128)}), f32[50,512]{1,0:T(8,128)}) %all-reduce.2.cloned.1.call-update) | async-done | bytes 102416 | tf_op jit(solution)/shard_map/psum | solution.py:48
  1267.3 1.6 broadcast_divide_fusion
  (4 shorter events, 0.0 us)
Async XLA Ops:
  7.2 78.0 %all-gather.2.cloned.1.call-start = ((), (), s32[]{:S(2)}) async-start(), calls=%async_computation | async-start | bytes 1863680 | tf_op jit(solution)/shard_map/all_gather | solution.py:29
  7.9 1259.4 %all-reduce.2.cloned.1.call-start = ((), (), s32[]{:S(2)}) async-start(), calls=%async_computation.1 | async-start | bytes 229376 | tf_op jit(solution)/shard_map/psum | solution.py:48
  86.9 47.1 %copy-start.4 = (f32[512]{0:T(512)S(1)}, f32[512]{0:T(512)}, u32[]{:S(2)}) copy-start(f32[512]{0:T(512)} %param.6) | copy-start | bytes 6148
  133.9 474.8 %copy-start.2 = (f32[8192]{0:T(1024)S(1)}, f32[8192]{0:T(1024)}, u32[]{:S(2)}) copy-start(f32[8192]{0:T(1024)} %param.7) | copy-start | bytes 98308
  643.1 264.1 %copy-start.3 = (f32[512]{0:T(512)}, f32[512]{0:T(512)S(1)}, u32[]{:S(2)}) copy-start(f32[512]{0:T(512)S(1)} %multiply_subtract_fusion.3) | copy-start | bytes 6148
  897.6 273.2 %copy-start = (f32[50,8192]{1,0:T(8,128)S(1)}, f32[50,8192]{1,0:T(8,128)}, u32[]{:S(2)}) copy-start(f32[50,8192]{1,0:T(8,128)} %all-gather.2.cloned.1.call-done) | copy-start | bytes 4915204
  1153.3 40.4 %copy-start.1 = (f32[8192]{0:T(1024)}, f32[8192]{0:T(1024)S(1)}, u32[]{:S(2)}) copy-start(f32[8192]{0:T(1024)S(1)} %multiply_subtract_fusion.1) | copy-start | bytes 98308
Sparse Core Ops, SparseCore 0:
  10.6 74.5 all-gather.1
  1193.8 73.4 all-reduce.1
where the time goes:
time: 1280 us
  blocking collectives  1000 us (78%)
  waiting for transfers between devices  134 us (10%)
  other arithmetic  82.3 us (6%)
  matrix products  42.6 us (3%)
  between operations  14.4 us (1%)
    psum x2, blocking collectives, col_lse(): total = lax.psum(jnp.sum(jnp.exp(scores - top[None, :]), axis=0), 'cell')  492 us
    pmax x2, blocking collectives, col_lse(): top = lax.pmax(local_top, 'cell')  457 us
    all_gather x1, waiting for transfers between devices, on_device(): spots = lax.all_gather(spots_pca, 'cell', axis=1, tiled=True)  76.3 us
    psum x1, waiting for transfers between devices, on_device(): numer, total = lax.psum((numer, jnp.sum(weight, axis=1)), 'spot')  56.7 us
  transfers between devices with their start and end apart: 2, of which 2 were waited for; matrix products, arithmetic and copies ran while one was open for 1% of the time, Pallas kernels for 0%

commit v1 on v0

v1 whole, which is shorter than its diff:
```python
import math

import jax
import jax.numpy as jnp
from jax import lax
from jax.experimental import pallas as pl
from jax.experimental.pallas import tpu as pltpu
from jax.sharding import PartitionSpec as P

MESH = pl.DeviceIdType.MESH
F32, BF16 = jnp.float32, jnp.bfloat16

PC = 50
ROWS = 56
SEC = 64
TILE = 2048
BLK = 512
HALF = TILE // 2
SPT = 128
RB = 256
blur = 0.25
LOG2E = math.log2(math.e)
SCALE = LOG2E / blur
UNSCALE = blur / LOG2E


def pieces3(v):
    one = v.astype(BF16).astype(F32)
    rest = v - one
    two = rest.astype(BF16).astype(F32)
    return one, two, (rest - two).astype(BF16).astype(F32)


def pad_rows(v, rows):
    return jnp.concatenate([v, jnp.zeros((rows - v.shape[0], v.shape[1]), v.dtype)], axis=0)


def lse(v, axis):
    top = jnp.max(v, axis=axis, keepdims=True)
    out = top + jnp.log2(jnp.sum(jnp.exp2(v - top), axis=axis, keepdims=True))
    return out


def kernel(
    cells_ref, spots_ref, loga_ref, logb_ref, outf_ref, outg_ref, outb_ref,
    cg, lab, lbb, sg, ab, bb, at, e, run, ucol, urow, rb1, rb2, cs1, cr1, cz1, gh1, cs2, cr2, cz2, gh2, gbuf, stage, rs, ag,
    pot, fo, tops, sums, qrow, ptb, bt, xsum,
    l_in, s_cell, r_cell, s_half, r_half, s_lab, r_lab, s_spot, r_spot, s_core, r_core, s_row1, r_row1, s_row2, r_row2,
    s_pair, r_pair, s_col1, r_col1, s_col2, r_col2, s_g, r_g, s_rs, r_rs, s_ag, r_ag, l_out,
):
    b = lax.axis_index("cell")
    x = lax.axis_index("spot")
    s = b & 15
    y, z, c = b // 16, s // 2, b & 1
    xy = x * 4 + y

    def dev(dx, dy, dz, dc):
        px, py, pz, pc = (x + dx) & 3, (y + dy) & 3, (z + dz) & 7, (c + dc) & 1
        return ((py * 8 + pz) * 2 + pc, px)

    row_peers = [(dx, dy, 0, 0) for dx in (2, 1, 3, 0) for dy in (2, 1, 3, 0) if dx or dy]
    ring = (4, 3, 5, 2, 6, 1, 7)
    ring_peers = [(0, 0, dz, 0) for dz in ring]
    sibling = (0, 0, 0, 1)
    peers = row_peers + ring_peers + [sibling]
    barrier = pltpu.get_barrier_semaphore()
    for peer in peers:
        pl.semaphore_signal(barrier, inc=1, device_id=dev(*peer), device_id_type=MESH)

    loads = [
        pltpu.make_async_copy(cells_ref.at[:, pl.ds(0, 256)], cg.at[y, 0], l_in.at[0]),
        pltpu.make_async_copy(cells_ref.at[:, pl.ds(256, 256)], cg.at[y, 1], l_in.at[1]),
        pltpu.make_async_copy(spots_ref, sg.at[s], l_in.at[2]),
        pltpu.make_async_copy(loga_ref, lab.at[y], l_in.at[3]),
        pltpu.make_async_copy(logb_ref.at[:, pl.ds(pl.multiple_of(y * TILE, TILE), TILE)], lbb, l_in.at[4]),
    ]
    for one in loads:
        one.start()
    run[0:8, :] = jnp.full((8, TILE), -jnp.inf, F32)
    run[8:16, :] = jnp.zeros((8, TILE), F32)
    for one in loads:
        one.wait()
    pl.semaphore_wait(barrier, len(peers))

    sends = []

    def copy(src, dst, ssem, rsem, peer):
        return pltpu.make_async_remote_copy(
            src_ref=src, dst_ref=dst, send_sem=ssem, recv_sem=rsem, device_id=dev(*peer), device_id_type=MESH
        )

    def start(*args):
        one = copy(*args)
        one.start()
        sends.append(one)
        return one

    def arrive(copies):
        for one in copies:
            one.wait_recv()

    near = {}
    for dy in (1, 3):
        for h in (0, 1) if dy == 1 else (1, 0):
            ref = cg.at[y, h]
            near[dy, h] = start(ref, ref, s_cell.at[dy, h], r_cell.at[dy, h], (0, dy, 0, 0))

    def turn(p):
        return jnp.where((p & 1) == 1, (p + 1) // 2, 8 - p // 2)

    def slot_of(p, other):
        return ((z + 8 - turn(p)) & 7) * 2 + (1 - c if other else c)

    def ring_copy(p):
        ref = sg.at[s]
        return copy(ref, ref, s_spot.at[p], r_spot.at[p], (0, 0, turn(p), 0))

    def hand_on(p):
        ref = sg.at[slot_of(p, False)]
        return copy(ref, ref, s_core.at[p], r_core.at[p], sibling)

    own = sg.at[s]
    pair0 = start(own, own, s_core.at[0], r_core.at[0], sibling)
    lax.fori_loop(1, 8, lambda p, carry: (ring_copy(p).start(), carry)[1], 0)
    lab_in = [start(lab.at[y], lab.at[y], s_lab.at[dy], r_lab.at[dy], (0, dy, 0, 0)) for dy in (1, 2, 3)]

    row = lax.broadcasted_iota(jnp.int32, (ROWS, 1), 0)
    centre = jnp.sum(sg[s], axis=1, keepdims=True) * (1.0 / SPT)

    def stack(v, extra, order):
        hi = v.astype(BF16)
        lo = (v - hi.astype(F32)).astype(BF16)
        first = pad_rows((hi.astype(F32) + extra).astype(BF16), SEC)
        hi, lo = pad_rows(hi, SEC), pad_rows(lo, SEC)
        return jnp.concatenate([first] + [(hi, lo)[k] for k in order], axis=0)

    def prep_cells(yy, h):
        lanes = pl.ds(pl.multiple_of(yy * BLK + h * 256, 256), 256)
        v = pad_rows(cg[yy, h] - centre, ROWS)
        pot[0:1, lanes] = jnp.sum(v * v, axis=0, keepdims=True) * SCALE
        extra = jnp.where((row >= PC) & (row < PC + 3), 1.0, 0.0) + jnp.zeros((ROWS, 256), F32)
        ab[:, lanes] = stack(v * (2.0 * SCALE), extra, (0, 1, 1))

    def prep_spots(slot):
        v = pad_rows(sg[slot] - centre, ROWS)
        norm = jnp.sum(v * v, axis=0, keepdims=True) * (-SCALE)
        n1, n2, n3 = pieces3(norm)
        extra = jnp.where(row == PC, n1, 0.0) + jnp.where(row == PC + 1, n2, 0.0) + jnp.where(row == PC + 2, n3, 0.0)
        extra = extra + jnp.where((row >= PC + 3) & (row < PC + 6), 1.0, 0.0)
        block = stack(v, extra, (1, 0, 1))
        bb[:, pl.ds(pl.multiple_of(slot * SPT, SPT), SPT)] = block
        bt[pl.ds(pl.multiple_of(slot * SPT, SPT), SPT), :] = block.T

    def update(slot, yy):
        lanes = pl.ds(pl.multiple_of(yy * BLK, BLK), BLK)
        left = bt[pl.ds(pl.multiple_of(slot * SPT, SPT), SPT), :]
        t = jnp.dot(left, ab[:, lanes], preferred_element_type=F32).reshape(SPT // 8, 8, BLK)
        old = run[0:8, lanes]
        top = jnp.maximum(old, jnp.max(t, axis=0))
        run[8:16, lanes] = run[8:16, lanes] * jnp.exp2(old - top) + jnp.sum(jnp.exp2(t - top[None]), axis=0)
        run[0:8, lanes] = top

    def stream(slots, offsets, fresh=True):
        if fresh:
            for slot in slots:
                prep_spots(slot)
        for slot in slots:
            for dy in offsets:
                update(slot, (y + dy) & 3)

    def got(p):
        ring_copy(p).wait_recv()
        hand_on(p).start()

    prep_cells(y, 0)
    prep_cells(y, 1)
    below, above = (y + 3) & 3, (y + 1) & 3
    near[1, 0].wait_recv()
    ref = cg.at[below, 0]
    far0 = start(ref, ref, s_half.at[0], r_half.at[0], (0, 1, 0, 0))
    near[3, 1].wait_recv()
    ref = cg.at[above, 1]
    far1 = start(ref, ref, s_half.at[1], r_half.at[1], (0, 3, 0, 0))
    prep_cells(below, 0)
    prep_cells(above, 1)
    near[1, 1].wait_recv()
    prep_cells(below, 1)
    near[3, 0].wait_recv()
    prep_cells(above, 0)

    got(1)
    got(2)
    pair0.wait_recv()
    stream([s, z * 2 + 1 - c, slot_of(1, False), slot_of(2, False)], (0, 1, 3))

    def four(k, carry):
        got(2 * k + 1)
        got(2 * k + 2)
        hand_on(2 * k - 1).wait_recv()
        hand_on(2 * k).wait_recv()
        stream(
            [slot_of(2 * k - 1, True), slot_of(2 * k, True), slot_of(2 * k + 1, False), slot_of(2 * k + 2, False)],
            (0, 1, 3),
        )
        return carry

    lax.fori_loop(1, 3, four, 0)
    arrive([far0, far1])
    yy = (y + 2) & 3
    prep_cells(yy, 0)
    prep_cells(yy, 1)
    stream([s, z * 2 + 1 - c] + [slot_of(p, False) for p in (1, 2, 3, 4)], (2,), False)
    got(7)
    stream([slot_of(p, True) for p in (1, 2, 3, 4)] + [slot_of(p, False) for p in (5, 6)], (2,), False)
    hand_on(5).wait_recv()
    hand_on(6).wait_recv()
    stream([slot_of(7, False), slot_of(5, True), slot_of(6, True)], (0, 1, 3, 2))
    hand_on(7).wait_recv()
    stream([slot_of(7, True)], (0, 1, 3, 2))
    top = jnp.max(run[0:8, :], axis=0, keepdims=True)
    total = jnp.sum(run[8:16, :] * jnp.exp2(run[0:8, :] - top), axis=0, keepdims=True)
    rb1[xy] = top + jnp.log2(total) - pot[0:1, :]

    def row_exchange(buf, ssem, rsem):
        return [start(buf.at[xy], buf.at[xy], ssem.at[k], rsem.at[k], peer) for k, peer in enumerate(row_peers)]

    moving = row_exchange(rb1, s_row1, r_row1)
    for k in range(TILE // 256):
        at[k * 256 : (k + 1) * 256, :] = ab[:, k * 256 : (k + 1) * 256].T
    arrive(lab_in)
    for k in range(4):
        pot[1:2, k * BLK : (k + 1) * BLK] = lab[k] * LOG2E
    arrive(moving)
    cell1 = pot[1:2, :] - lse(rb1[...], 0)[0]
    pot[2:3, :] = cell1
    f1, f2, f3 = pieces3(cell1 - pot[0:1, :])
    urow[0:1, :] = f1
    urow[1:2, :] = f2
    urow[2:3, :] = f3
    urow[3:8, :] = jnp.zeros((5, TILE), F32)
    lane = lax.broadcasted_iota(jnp.int32, (8, 128), 1)
    sub = lax.broadcasted_iota(jnp.int32, (8, 128), 0)
    pick = jnp.where((lane == sub + PC + 3) & (sub < 3), 1.0, 0.0)
    spread = lax.dot_general(
        urow[...].astype(BF16), pick.astype(BF16), (((0,), (0,)), ((), ())), preferred_element_type=F32
    )
    at[:, 0:128] = (at[:, 0:128].astype(F32) + spread).astype(BF16)

    def half_lanes(h):
        return pl.ds(pl.multiple_of(h * HALF, HALF), HALF)

    def col_pass(h):
        lanes = half_lanes(h)
        right = bb[:, lanes]
        for r in range(TILE // RB):
            t = jnp.dot(at[r * RB : (r + 1) * RB, :], right, preferred_element_type=F32)
            top = jnp.max(jnp.max(t.reshape(RB // 8, 8, HALF), axis=0), axis=0, keepdims=True)
            w = jnp.exp2(t - top)
            e[h, r * RB : (r + 1) * RB, :] = w
            tops[r : r + 1, lanes] = top
            sums[r : r + 1, lanes] = jnp.sum(jnp.sum(w.reshape(RB // 8, 8, HALF), axis=0), axis=0, keepdims=True)
        return lse(tops[:, lanes] + jnp.log2(sums[:, lanes]), 0)

    def ring_exchange(buf, ssem, rsem):
        return [start(buf.at[z], buf.at[z], ssem.at[k], rsem.at[k], peer) for k, peer in enumerate(ring_peers)]

    cs1[...] = col_pass(1 - c)
    half = start(cs1, cr1, s_pair.at[0], r_pair.at[0], sibling)
    mine = col_pass(c)
    half.wait_recv()
    cz1[z] = lse(jnp.concatenate([mine, cr1[...]], axis=0), 0)
    arrive(ring_exchange(cz1, s_col1, r_col1))
    gh1[c] = lbb[:, half_lanes(c)] * LOG2E - lse(cz1[...], 0)[0]
    back = start(gh1.at[c], gh1.at[c], s_pair.at[1], r_pair.at[1], sibling)

    def scales(h):
        q = jnp.exp2(tops[:, half_lanes(h)] + gh1[h])
        for r in range(TILE // RB):
            qrow[h, r] = q[r : r + 1]

    def row_sums(h, last):
        def step(r, carry):
            for k in (0, 1):
                rows = pl.ds(pl.multiple_of(r * RB + k * 128, 128), 128)
                t = ucol[rows, :] if last else jnp.zeros((128, 128), F32)
                for j in range(HALF // 128):
                    lanes = slice(j * 128, (j + 1) * 128)
                    w = e[h, rows, lanes] * qrow[h, r, :, lanes]
                    e[h, rows, lanes] = w
                    t = t + w
                if last:
                    rb2[xy, :, rows] = jnp.sum(t.T, axis=0, keepdims=True)
                else:
                    ucol[rows, :] = t
            return carry

        lax.fori_loop(0, TILE // RB, step, 0)

    scales(c)
    row_sums(c, False)
    back.wait_recv()
    scales(1 - c)
    row_sums(1 - c, True)
    arrive(row_exchange(rb2, s_row2, r_row2))
    ratio = jnp.exp2(pot[1:2, :]) / jnp.sum(rb2[...], axis=0)
    u1, u2, u3 = pieces3(ratio)
    urow[0:1, :] = u1
    urow[1:2, :] = u2
    urow[2:3, :] = u3
    ones = jnp.where(sub < 3, 1.0, 0.0)
    ucol[...] = lax.dot_general(
        urow[...].astype(BF16), ones.astype(BF16), (((0,), (0,)), ((), ())), preferred_element_type=F32
    )

    def col_sums(h):
        def step(r, t):
            out = list(t)
            for q in range(8):
                rows = pl.ds(pl.multiple_of(r * 64 + q * 8, 8), 8)
                scale = ucol[rows, :]
                for k in range(HALF // 128):
                    out[k] = out[k] + e[h, rows, k * 128 : (k + 1) * 128] * scale
            return tuple(out)

        parts = lax.fori_loop(0, TILE // 64, step, tuple(jnp.zeros((8, 128), F32) for k in range(HALF // 128)))
        return jnp.sum(jnp.concatenate(parts, axis=1), axis=0, keepdims=True)

    cs2[...] = col_sums(1 - c)
    half = start(cs2, cr2, s_pair.at[2], r_pair.at[2], sibling)
    mine = col_sums(c)
    half.wait_recv()
    cz2[z] = mine + cr2[...]
    moving = ring_exchange(cz2, s_col2, r_col2)
    fo[...] = (pot[2:3, :] + jnp.log2(ratio)) * UNSCALE
    out_f = pltpu.make_async_copy(fo.at[:, pl.ds(pl.multiple_of(y * BLK, BLK), BLK)], outf_ref, l_out.at[0])
    out_f.start()
    arrive(moving)
    gh2[c] = jnp.exp2(lbb[:, half_lanes(c)] * LOG2E) / jnp.sum(cz2[...], axis=0)
    back = start(gh2.at[c], gh2.at[c], s_pair.at[3], r_pair.at[3], sibling)

    def weigh(h):
        for k in range(8):
            lanes = slice(k * SPT, (k + 1) * SPT)
            v = jnp.where(row == PC, 1.0, pad_rows(sg[h * 8 + k], ROWS)) * gh2[h, :, lanes]
            hi = v.astype(BF16)
            ptb[h, 0:SEC, lanes] = pad_rows(hi, SEC)
            ptb[h, SEC : 2 * SEC, lanes] = pad_rows((v - hi.astype(F32)).astype(BF16), SEC)

    contract = (((1,), (1,)), ((), ()))

    def product(dy, h):
        w = e[h, pl.ds(pl.multiple_of(((y + dy) & 3) * BLK, BLK), BLK), :]
        hi = w.astype(BF16)
        lo = (w - hi.astype(F32)).astype(BF16)
        part = lax.dot_general(hi, ptb[h], contract, preferred_element_type=F32)
        return part + lax.dot_general(lo, ptb[h], contract, preferred_element_type=F32)

    along_x, along_y, g_in = {}, [], []

    def send_x(dy, part):
        part = part.T
        part = (part[0:ROWS] + part[SEC : SEC + ROWS])[0 : PC + 1]
        for k in range(4):
            stage[dy * 4 + k] = part[:, k * SPT : (k + 1) * SPT]
        along_x[dy] = []
        for dx in (2, 1, 3):
            k = dy * 4 + dx
            src, dst = stage.at[dy * 4 + ((x + dx) & 3)], rs.at[k]
            along_x[dy].append(start(src, dst, s_rs.at[k], r_rs.at[k], (dx, 0, 0, 0)))

    def send_y(dy):
        arrive(along_x[dy])
        k = dy * 4
        xsum[dy] = (stage[k + x] + rs[k + 1]) + (rs[k + 2] + rs[k + 3])
        if dy:
            along_y.append(start(xsum.at[dy], rs.at[k], s_rs.at[k], r_rs.at[k], (0, dy, 0, 0)))

    weigh(c)
    first = product(2, c)
    back.wait_recv()
    weigh(1 - c)
    send_x(2, first + product(2, 1 - c))
    for h in (0, 1):
        gbuf[y, :, h * HALF : (h + 1) * HALF] = (gh1[h] + jnp.log2(gh2[h])) * UNSCALE
    send_x(1, product(1, c) + product(1, 1 - c))
    send_x(3, product(3, c) + product(3, 1 - c))
    send_y(2)
    send_x(0, product(0, c) + product(0, 1 - c))
    for dy in (2, 1, 3):
        g_in.append(start(gbuf.at[y], gbuf.at[y], s_g.at[dy], r_g.at[dy], (0, dy, 0, 0)))
    send_y(1)
    send_y(3)
    send_y(0)
    arrive(g_in)
    outs = [
        pltpu.make_async_copy(gbuf.at[k], outg_ref.at[:, pl.ds(k * TILE, TILE)], l_out.at[1 + k]) for k in range(4)
    ]
    for one in outs:
        one.start()
    arrive(along_y)
    whole = (xsum[0] + rs[4]) + (rs[8] + rs[12])
    ag[x] = whole[0:PC] / whole[PC : PC + 1, :]
    mine = ag.at[x]
    ag_in = [start(mine, mine, s_ag.at[dx], r_ag.at[dx], (dx, 0, 0, 0)) for dx in (2, 1, 3)]
    arrive(ag_in)
    for k in range(4):
        outs.append(
            pltpu.make_async_copy(ag.at[k], outb_ref.at[:, pl.ds(k * SPT, SPT)], l_out.at[5 + k])
        )
        outs[-1].start()
    for one in sends:
        one.wait_send()

    def drain(p, carry):
        ring_copy(p).wait_send()
        hand_on(p).wait_send()
        return carry

    lax.fori_loop(1, 8, drain, 0)
    for one in [out_f] + outs:
        one.wait()


def settle(f_ref, g_ref, b_ref, outf_ref, outg_ref, outb_ref):
    outf_ref[...] = f_ref[...]
    outg_ref[...] = g_ref[...]
    outb_ref[...] = b_ref[...]


def on_device(cells_pca, spots_pca, log_a, log_b):
    dma = pltpu.SemaphoreType.DMA
    hbm = pl.BlockSpec(memory_space=pl.ANY)
    vmem = pl.BlockSpec(memory_space=pltpu.VMEM)
    shapes = (
        jax.ShapeDtypeStruct((1, BLK), F32),
        jax.ShapeDtypeStruct((1, 4 * TILE), F32),
        jax.ShapeDtypeStruct((PC, BLK), F32),
    )
    pairs = ((4, 2), (2,), (4,), (8,), (8,), (15,), (15,), (4,), (7,), (7,), (4,), (16,), (4,))
    out = pl.pallas_call(
        kernel,
        out_shape=shapes,
        in_specs=[hbm] * 4,
        out_specs=(hbm,) * 3,
        scratch_shapes=[
            pltpu.VMEM((4, 2, PC, 256), F32),
            pltpu.VMEM((4, 1, BLK), F32),
            pltpu.VMEM((1, TILE), F32),
            pltpu.VMEM((16, PC, SPT), F32),
            pltpu.VMEM((4 * SEC, TILE), BF16),
            pltpu.VMEM((4 * SEC, TILE), BF16),
            pltpu.VMEM((TILE, 4 * SEC), BF16),
            pltpu.VMEM((2, TILE, HALF), F32),
            pltpu.VMEM((16, TILE), F32),
            pltpu.VMEM((TILE, 128), F32),
            pltpu.VMEM((8, TILE), F32),
            pltpu.VMEM((16, 1, TILE), F32),
            pltpu.VMEM((16, 1, TILE), F32),
            pltpu.VMEM((1, HALF), F32),
            pltpu.VMEM((1, HALF), F32),
            pltpu.VMEM((8, 1, HALF), F32),
            pltpu.VMEM((2, 1, HALF), F32),
            pltpu.VMEM((1, HALF), F32),
            pltpu.VMEM((1, HALF), F32),
            pltpu.VMEM((8, 1, HALF), F32),
            pltpu.VMEM((2, 1, HALF), F32),
            pltpu.VMEM((4, 1, TILE), F32),
            pltpu.VMEM((16, PC + 1, SPT), F32),
            pltpu.VMEM((16, PC + 1, SPT), F32),
            pltpu.VMEM((4, PC, SPT), F32),
            pltpu.VMEM((8, TILE), F32),
            pltpu.VMEM((1, TILE), F32),
            pltpu.VMEM((TILE // RB, TILE), F32),
            pltpu.VMEM((TILE // RB, TILE), F32),
            pltpu.VMEM((2, TILE // RB, 1, HALF), F32),
            pltpu.VMEM((2, 2 * SEC, HALF), BF16),
            pltpu.VMEM((TILE, 4 * SEC), BF16),
            pltpu.VMEM((4, PC + 1, SPT), F32),
            dma((5,)),
        ]
        + [dma(n) for n in pairs for _ in range(2)]
        + [dma((9,))],
        compiler_params=pltpu.CompilerParams(
            collective_id=0, has_side_effects=True, vmem_limit_bytes=58 * 2**20
        ),
        cost_estimate=pl.CostEstimate(flops=10 * 2**30, bytes_accessed=2**20, transcendentals=2**23),
        name="sinkhorn",
    )(cells_pca, spots_pca, log_a.reshape(1, BLK), log_b.reshape(1, 4 * TILE))
    f, g, bary = pl.pallas_call(
        settle,
        out_shape=shapes,
        in_specs=[vmem] * 3,
        out_specs=(vmem,) * 3,
        name="settle",
    )(*out)
    return f.reshape(BLK), g.reshape(4 * TILE), bary


def solution(mesh):
    placed = (P(None, "cell"), P(None, ("spot", "cell")), P("cell"), P("spot"))
    return jax.shard_map(
        on_device,
        mesh=mesh,
        in_specs=placed,
        out_specs=(P("cell"), P("spot"), P(None, "cell")),
        check_vma=False,
    )
```

time: 1280 us -> 71.1 us (0.06)
  blocking collectives: 1000 us -> 0 us
  waiting for transfers between devices: 134 us -> 0 us
  other arithmetic: 82.3 us -> 0 us
  Pallas kernels: 0 us -> 70.3 us
  matrix products: 42.6 us -> 0 us
  between operations: 14.4 us -> 0.64 us
    psum x5 -> x0, blocking collectives: 516 us -> none  [the longest x2 492 us: col_lse(): total = lax.psum(jnp.sum(jnp.exp(scores - top[None, :]), axis=0), 'cell')]
    pmax x5 -> x0, blocking collectives: 487 us -> none  [the longest x2 457 us: col_lse(): top = lax.pmax(local_top, 'cell')]
    all_gather x1 -> x0, waiting for transfers between devices: 76.3 us -> none  [on_device(): spots = lax.all_gather(spots_pca, 'cell', axis=1, tiled=True)]
    pallas_call x0 -> x2, Pallas kernels: none -> 70.3 us  [the longest x1 68.7 us: on_device(): pl.pallas_call(kernel, out_shape=shapes, in_specs=[hbm] * 4, out_specs=(h...]
    psum x1 -> x0, waiting for transfers between devices: 56.7 us -> none  [on_device(): numer, total = lax.psum((numer, jnp.sum(weight, axis=1)), 'spot')]
    reduce_sum x7 -> x0, other arithmetic: 49 us -> none  [the longest x2 19 us: col_lse(): total = lax.psum(jnp.sum(jnp.exp(scores - top[None, :]), axis=0), 'cell')]
    dot_general x2 -> x0, matrix products: 42.6 us -> none  [the longest x1 22.8 us: on_device(): jnp.dot(spots, weight.T, precision=lax.Precision.HIGHEST, preferred_eleme...]
    reduce_max x4 -> x0, other arithmetic: 31.7 us -> none  [the longest x2 16.7 us: col_lse(): local_top = jnp.max(scores, axis=0)]
  transfers between devices with their start and end apart: 2 -> 0, of which waited for: 2 -> 0; matrix products, arithmetic and copies ran while one was open for 1% -> 0% of each run, Pallas kernels for 0% -> 0%
where the time goes in v1:
time: 71.1 us; the launch traced here: 70.9 us
  Pallas kernels  70.3 us (99%)
    pallas_call x1, Pallas kernels, on_device(): pl.pallas_call(kernel, out_shape=shapes, in_specs=[hbm] * 4, out_specs=(h...  68.7 us
    pallas_call x1, Pallas kernels, on_device(): pl.pallas_call(settle, out_shape=shapes, in_specs=[vmem] * 3, out_specs=(...  1.59 us

profile of v1, /device:TPU:24, one launch (start us, length us, event | category | flops | bytes accessed | tf_op | source)
XLA Modules:
  0.0 70.9 jit_solution(14662894783445520124)
XLA Ops:
  0.6 68.7 %sinkhorn.1 = (f32[1,512]{1,0:T(1,128)}, f32[1,8192]{1,0:T(1,128)}, f32[50,512]{1,0:T(8,128)}) custom-call(f32[50,512]{1,0:T(8,128)} %cells_ref.1, f32[50,128]{1,0:T(8,128)} %spots_ref.1, f32[1,512]{1,0:T(1,128)} %bitcast.6, f32[1,8192]{1,0:T(1,128)} %bitcast.4), custom_call_target="tpu_custom_call" | custom-call | flops 10737418240 | bytes 1048576 | tf_op jit(solution)/shard_map/sinkhorn/pallas_call | solution.py:440
  69.4 1.6 %settle.1 = (f32[1,512]{1,0:T(1,128)}, f32[1,8192]{1,0:T(1,128)}, f32[50,512]{1,0:T(8,128)}) custom-call(f32[1,512]{1,0:T(1,128)} %get-tuple-element.9.f_ref, f32[1,8192]{1,0:T(1,128)} %get-tuple-element.10.g_ref, f32[50,512]{1,0:T(8,128)} %get-tuple-element.11.b_ref), custom_call_target="tpu_custom_call" | custom-call | tf_op jit(solution)/shard_map/settle/pallas_call | solution.py:489

commit v2 on v1

--- a/solution.py
+++ b/solution.py
@@ -17,7 +17,7 @@
 BLK = 512
 HALF = TILE // 2
 SPT = 128
-RB = 256
+RB = 128
 blur = 0.25
 LOG2E = math.log2(math.e)
 SCALE = LOG2E / blur
@@ -44,7 +44,7 @@
 def kernel(
     cells_ref, spots_ref, loga_ref, logb_ref, outf_ref, outg_ref, outb_ref,
     cg, lab, lbb, sg, ab, bb, at, e, run, ucol, urow, rb1, rb2, cs1, cr1, cz1, gh1, cs2, cr2, cz2, gh2, gbuf, stage, rs, ag,
-    pot, fo, tops, sums, qrow, ptb, bt, xsum,
+    pot, fo, tops, sums, qrow, ptb, eh, el, bt, xsum,
     l_in, s_cell, r_cell, s_half, r_half, s_lab, r_lab, s_spot, r_spot, s_core, r_core, s_row1, r_row1, s_row2, r_row2,
     s_pair, r_pair, s_col1, r_col1, s_col2, r_col2, s_g, r_g, s_rs, r_rs, s_ag, r_ag, l_out,
 ):
@@ -227,6 +227,10 @@
     moving = row_exchange(rb1, s_row1, r_row1)
     for k in range(TILE // 256):
         at[k * 256 : (k + 1) * 256, :] = ab[:, k * 256 : (k + 1) * 256].T
+    for h in (0, 1):
+        for r in range(TILE // 256):
+            rows = slice(r * 256, (r + 1) * 256)
+            e[h, rows, :] = jnp.dot(at[rows, :], bb[:, h * HALF : (h + 1) * HALF], preferred_element_type=F32)
     arrive(lab_in)
     for k in range(4):
         pot[1:2, k * BLK : (k + 1) * BLK] = lab[k] * LOG2E
@@ -238,28 +242,40 @@
     urow[1:2, :] = f2
     urow[2:3, :] = f3
     urow[3:8, :] = jnp.zeros((5, TILE), F32)
-    lane = lax.broadcasted_iota(jnp.int32, (8, 128), 1)
     sub = lax.broadcasted_iota(jnp.int32, (8, 128), 0)
-    pick = jnp.where((lane == sub + PC + 3) & (sub < 3), 1.0, 0.0)
-    spread = lax.dot_general(
-        urow[...].astype(BF16), pick.astype(BF16), (((0,), (0,)), ((), ())), preferred_element_type=F32
-    )
-    at[:, 0:128] = (at[:, 0:128].astype(F32) + spread).astype(BF16)
+    ones = jnp.where(sub < 3, 1.0, 0.0).astype(BF16)
+
+    def to_column():
+        return lax.dot_general(
+            urow[...].astype(BF16), ones, (((0,), (0,)), ((), ())), preferred_element_type=F32
+        )
+
+    ucol[...] = to_column()
 
     def half_lanes(h):
         return pl.ds(pl.multiple_of(h * HALF, HALF), HALF)
 
     def col_pass(h):
-        lanes = half_lanes(h)
-        right = bb[:, lanes]
-        for r in range(TILE // RB):
-            t = jnp.dot(at[r * RB : (r + 1) * RB, :], right, preferred_element_type=F32)
-            top = jnp.max(jnp.max(t.reshape(RB // 8, 8, HALF), axis=0), axis=0, keepdims=True)
-            w = jnp.exp2(t - top)
-            e[h, r * RB : (r + 1) * RB, :] = w
-            tops[r : r + 1, lanes] = top
-            sums[r : r + 1, lanes] = jnp.sum(jnp.sum(w.reshape(RB // 8, 8, HALF), axis=0), axis=0, keepdims=True)
-        return lse(tops[:, lanes] + jnp.log2(sums[:, lanes]), 0)
+        def step(r, carry):
+            for q in range(2):
+                at_r = r * 2 + q
+                rows = pl.ds(pl.multiple_of(at_r * RB, RB), RB)
+                f = ucol[rows, :]
+                for k in range(HALF // 128):
+                    lanes = slice(k * 128, (k + 1) * 128)
+                    v = (e[h, rows, lanes] + f).reshape(RB // 8, 8, 128)
+                    top = jnp.max(v, axis=0)
+                    w = jnp.exp2(v - top[None])
+                    e[h, rows, lanes] = w.reshape(RB, 128)
+                    tops[h, at_r, :, lanes] = top
+                    sums[at_r, :, lanes] = jnp.sum(w, axis=0)
+            return carry
+
+        lax.fori_loop(0, TILE // 256, step, 0)
+        part = tops[h].reshape(TILE // RB * 8, HALF)
+        top = jnp.max(part, axis=0, keepdims=True)
+        total = jnp.sum(sums[...].reshape(TILE // RB * 8, HALF) * jnp.exp2(part - top), axis=0, keepdims=True)
+        return top + jnp.log2(total)
 
     def ring_exchange(buf, ssem, rsem):
         return [start(buf.at[z], buf.at[z], ssem.at[k], rsem.at[k], peer) for k, peer in enumerate(ring_peers)]
@@ -274,55 +290,56 @@
     back = start(gh1.at[c], gh1.at[c], s_pair.at[1], r_pair.at[1], sibling)
 
     def scales(h):
-        q = jnp.exp2(tops[:, half_lanes(h)] + gh1[h])
-        for r in range(TILE // RB):
-            qrow[h, r] = q[r : r + 1]
+        qrow[h] = jnp.exp2(tops[h] + gh1[h])
 
     def row_sums(h, last):
         def step(r, carry):
-            for k in (0, 1):
-                rows = pl.ds(pl.multiple_of(r * RB + k * 128, 128), 128)
-                t = ucol[rows, :] if last else jnp.zeros((128, 128), F32)
-                for j in range(HALF // 128):
-                    lanes = slice(j * 128, (j + 1) * 128)
-                    w = e[h, rows, lanes] * qrow[h, r, :, lanes]
-                    e[h, rows, lanes] = w
-                    t = t + w
-                if last:
-                    rb2[xy, :, rows] = jnp.sum(t.T, axis=0, keepdims=True)
-                else:
-                    ucol[rows, :] = t
+            q = [qrow[h, r, :, j * 128 : (j + 1) * 128] for j in range(HALF // 128)]
+            block = pl.ds(pl.multiple_of(r * RB, RB), RB)
+            before = ucol[block, :] if last else None
+            out = []
+            for g in range(RB // 8):
+                rows = pl.ds(pl.multiple_of(r * RB + g * 8, 8), 8)
+                t = [e[h, rows, j * 128 : (j + 1) * 128] * q[j] for j in range(HALF // 128)]
+                while len(t) > 1:
+                    t = [t[j] + t[j + 1] for j in range(0, len(t), 2)]
+                out.append(t[0])
+            out = jnp.concatenate(out, axis=0)
+            ucol[block, :] = before + out if last else out
             return carry
 
         lax.fori_loop(0, TILE // RB, step, 0)
+
+    def to_row():
+        for k in range(TILE // 128):
+            rows = slice(k * 128, (k + 1) * 128)
+            rb2[xy, :, rows] = jnp.sum(ucol[rows, :].T, axis=0, keepdims=True)
 
     scales(c)
     row_sums(c, False)
     back.wait_recv()
     scales(1 - c)
     row_sums(1 - c, True)
+    to_row()
     arrive(row_exchange(rb2, s_row2, r_row2))
     ratio = jnp.exp2(pot[1:2, :]) / jnp.sum(rb2[...], axis=0)
     u1, u2, u3 = pieces3(ratio)
     urow[0:1, :] = u1
     urow[1:2, :] = u2
     urow[2:3, :] = u3
-    ones = jnp.where(sub < 3, 1.0, 0.0)
-    ucol[...] = lax.dot_general(
-        urow[...].astype(BF16), ones.astype(BF16), (((0,), (0,)), ((), ())), preferred_element_type=F32
-    )
+    ucol[...] = to_column()
 
     def col_sums(h):
         def step(r, t):
-            out = list(t)
-            for q in range(8):
-                rows = pl.ds(pl.multiple_of(r * 64 + q * 8, 8), 8)
+            out = [jnp.zeros((8, 128), F32) for k in t]
+            for g in range(RB // 8):
+                rows = pl.ds(pl.multiple_of(r * RB + g * 8, 8), 8)
                 scale = ucol[rows, :]
                 for k in range(HALF // 128):
                     out[k] = out[k] + e[h, rows, k * 128 : (k + 1) * 128] * scale
-            return tuple(out)
-
-        parts = lax.fori_loop(0, TILE // 64, step, tuple(jnp.zeros((8, 128), F32) for k in range(HALF // 128)))
+            return tuple(t[k] + out[k] * qrow[h, r, :, k * 128 : (k + 1) * 128] for k in range(HALF // 128))
+
+        parts = lax.fori_loop(0, TILE // RB, step, tuple(jnp.zeros((8, 128), F32) for k in range(HALF // 128)))
         return jnp.sum(jnp.concatenate(parts, axis=1), axis=0, keepdims=True)
 
     cs2[...] = col_sums(1 - c)
@@ -334,6 +351,19 @@
     fo[...] = (pot[2:3, :] + jnp.log2(ratio)) * UNSCALE
     out_f = pltpu.make_async_copy(fo.at[:, pl.ds(pl.multiple_of(y * BLK, BLK), BLK)], outf_ref, l_out.at[0])
     out_f.start()
+
+    def halve(r, carry):
+        rows = pl.ds(pl.multiple_of(r * RB, RB), RB)
+        for h in (0, 1):
+            for j in range(HALF // 256):
+                lanes = slice(j * 256, (j + 1) * 256)
+                w = (e[h, rows, lanes].reshape(RB // 8, 8, 256) * qrow[h, r, :, lanes][None]).reshape(RB, 256)
+                hi = w.astype(BF16)
+                eh[h, rows, lanes] = hi
+                el[h, rows, lanes] = (w - hi.astype(F32)).astype(BF16)
+        return carry
+
+    lax.fori_loop(0, TILE // RB, halve, 0)
     arrive(moving)
     gh2[c] = jnp.exp2(lbb[:, half_lanes(c)] * LOG2E) / jnp.sum(cz2[...], axis=0)
     back = start(gh2.at[c], gh2.at[c], s_pair.at[3], r_pair.at[3], sibling)
@@ -343,17 +373,13 @@
             lanes = slice(k * SPT, (k + 1) * SPT)
             v = jnp.where(row == PC, 1.0, pad_rows(sg[h * 8 + k], ROWS)) * gh2[h, :, lanes]
             hi = v.astype(BF16)
-            ptb[h, 0:SEC, lanes] = pad_rows(hi, SEC)
-            ptb[h, SEC : 2 * SEC, lanes] = pad_rows((v - hi.astype(F32)).astype(BF16), SEC)
-
-    contract = (((1,), (1,)), ((), ()))
+            lo = (v - hi.astype(F32)).astype(BF16)
+            ptb[h, lanes, :] = jnp.concatenate([pad_rows(hi, SEC), pad_rows(lo, SEC)], axis=0).T
 
     def product(dy, h):
-        w = e[h, pl.ds(pl.multiple_of(((y + dy) & 3) * BLK, BLK), BLK), :]
-        hi = w.astype(BF16)
-        lo = (w - hi.astype(F32)).astype(BF16)
-        part = lax.dot_general(hi, ptb[h], contract, preferred_element_type=F32)
-        return part + lax.dot_general(lo, ptb[h], contract, preferred_element_type=F32)
+        rows = pl.ds(pl.multiple_of(((y + dy) & 3) * BLK, BLK), BLK)
+        part = jnp.dot(eh[h, rows, :], ptb[h], preferred_element_type=F32)
+        return part + jnp.dot(el[h, rows, :], ptb[h], preferred_element_type=F32)
 
     along_x, along_y, g_in = {}, [], []
 
@@ -379,15 +405,19 @@
     first = product(2, c)
     back.wait_recv()
     weigh(1 - c)
-    send_x(2, first + product(2, 1 - c))
+    first = first + product(2, 1 - c)
+    second = product(1, c) + product(1, 1 - c)
+    send_x(2, first)
     for h in (0, 1):
         gbuf[y, :, h * HALF : (h + 1) * HALF] = (gh1[h] + jnp.log2(gh2[h])) * UNSCALE
-    send_x(1, product(1, c) + product(1, 1 - c))
-    send_x(3, product(3, c) + product(3, 1 - c))
-    send_y(2)
-    send_x(0, product(0, c) + product(0, 1 - c))
+    third = product(3, c) + product(3, 1 - c)
+    send_x(1, second)
     for dy in (2, 1, 3):
         g_in.append(start(gbuf.at[y], gbuf.at[y], s_g.at[dy], r_g.at[dy], (0, dy, 0, 0)))
+    fourth = product(0, c) + product(0, 1 - c)
+    send_x(3, third)
+    send_x(0, fourth)
+    send_y(2)
     send_y(1)
     send_y(3)
     send_y(0)
@@ -470,10 +500,12 @@
             pltpu.VMEM((4, PC, SPT), F32),
             pltpu.VMEM((8, TILE), F32),
             pltpu.VMEM((1, TILE), F32),
-            pltpu.VMEM((TILE // RB, TILE), F32),
-            pltpu.VMEM((TILE // RB, TILE), F32),
-            pltpu.VMEM((2, TILE // RB, 1, HALF), F32),
-            pltpu.VMEM((2, 2 * SEC, HALF), BF16),
+            pltpu.VMEM((2, TILE // RB, 8, HALF), F32),
+            pltpu.VMEM((TILE // RB, 8, HALF), F32),
+            pltpu.VMEM((2, TILE // RB, 8, HALF), F32),
+            pltpu.VMEM((2, HALF, 2 * SEC), BF16),
+            pltpu.VMEM((2, TILE, HALF), BF16),
+            pltpu.VMEM((2, TILE, HALF), BF16),
             pltpu.VMEM((TILE, 4 * SEC), BF16),
             pltpu.VMEM((4, PC + 1, SPT), F32),
             dma((5,)),

time: 71.1 us -> 68.8 us (0.968)
  Pallas kernels: 70.3 us -> 68 us
    pallas_call x1, Pallas kernels: 68.7 us -> 66.4 us  [on_device(): pl.pallas_call(kernel, out_shape=shapes, in_specs=[hbm] * 4, out_specs=(h...]
where the time goes in v2:
time: 68.8 us; the launch traced here: 68.6 us
  Pallas kernels  68 us (99%)
    pallas_call x1, Pallas kernels, on_device(): pl.pallas_call(kernel, out_shape=shapes, in_specs=[hbm] * 4, out_specs=(h...  66.4 us
    pallas_call x1, Pallas kernels, on_device(): pl.pallas_call(settle, out_shape=shapes, in_specs=[vmem] * 3, out_specs=(...  1.59 us

profile of v2, /device:TPU:24, one launch (start us, length us, event | category | flops | bytes accessed | tf_op | source)
XLA Modules:
  0.0 68.6 jit_solution(1102404625984226996)
XLA Ops:
  0.6 66.4 %sinkhorn.1 = (f32[1,512]{1,0:T(1,128)}, f32[1,8192]{1,0:T(1,128)}, f32[50,512]{1,0:T(8,128)}) custom-call(f32[50,512]{1,0:T(8,128)} %cells_ref.1, f32[50,128]{1,0:T(8,128)} %spots_ref.1, f32[1,512]{1,0:T(1,128)} %bitcast.6, f32[1,8192]{1,0:T(1,128)} %bitcast.4), custom_call_target="tpu_custom_call" | custom-call | flops 10737418240 | bytes 1048576 | tf_op jit(solution)/shard_map/sinkhorn/pallas_call | solution.py:470
  67.0 1.6 %settle.1 = (f32[1,512]{1,0:T(1,128)}, f32[1,8192]{1,0:T(1,128)}, f32[50,512]{1,0:T(8,128)}) custom-call(f32[1,512]{1,0:T(1,128)} %get-tuple-element.9.f_ref, f32[1,8192]{1,0:T(1,128)} %get-tuple-element.10.g_ref, f32[50,512]{1,0:T(8,128)} %get-tuple-element.11.b_ref), custom_call_target="tpu_custom_call" | custom-call | tf_op jit(solution)/shard_map/settle/pallas_call | solution.py:521

commit v3 on v2

--- a/solution.py
+++ b/solution.py
@@ -174,6 +174,9 @@
 
     prep_cells(y, 0)
     prep_cells(y, 1)
+    stream([s], (0,))
+    pair0.wait_recv()
+    stream([z * 2 + 1 - c], (0,))
     below, above = (y + 3) & 3, (y + 1) & 3
     near[1, 0].wait_recv()
     ref = cg.at[below, 0]
@@ -190,8 +193,8 @@
 
     got(1)
     got(2)
-    pair0.wait_recv()
-    stream([s, z * 2 + 1 - c, slot_of(1, False), slot_of(2, False)], (0, 1, 3))
+    stream([slot_of(1, False), slot_of(2, False)], (0, 1, 3))
+    stream([s, z * 2 + 1 - c], (1, 3), False)
 
     def four(k, carry):
         got(2 * k + 1)
@@ -412,32 +415,35 @@
         gbuf[y, :, h * HALF : (h + 1) * HALF] = (gh1[h] + jnp.log2(gh2[h])) * UNSCALE
     third = product(3, c) + product(3, 1 - c)
     send_x(1, second)
+    send_x(3, third)
+    fourth = product(0, c) + product(0, 1 - c)
+    send_x(0, fourth)
+    for dy in (2, 1, 3):
+        send_y(dy)
     for dy in (2, 1, 3):
         g_in.append(start(gbuf.at[y], gbuf.at[y], s_g.at[dy], r_g.at[dy], (0, dy, 0, 0)))
-    fourth = product(0, c) + product(0, 1 - c)
-    send_x(3, third)
-    send_x(0, fourth)
-    send_y(2)
-    send_y(1)
-    send_y(3)
     send_y(0)
+    arrive(along_y)
+    whole = (xsum[0] + rs[4]) + (rs[8] + rs[12])
+    ag[x] = whole[0:PC] / whole[PC : PC + 1, :]
+    mine = ag.at[x]
+    ag_in = [start(mine, mine, s_ag.at[dx], r_ag.at[dx], (dx, 0, 0, 0)) for dx in (2, 1, 3)]
     arrive(g_in)
     outs = [
         pltpu.make_async_copy(gbuf.at[k], outg_ref.at[:, pl.ds(k * TILE, TILE)], l_out.at[1 + k]) for k in range(4)
     ]
     for one in outs:
         one.start()
-    arrive(along_y)
-    whole = (xsum[0] + rs[4]) + (rs[8] + rs[12])
-    ag[x] = whole[0:PC] / whole[PC : PC + 1, :]
-    mine = ag.at[x]
-    ag_in = [start(mine, mine, s_ag.at[dx], r_ag.at[dx], (dx, 0, 0, 0)) for dx in (2, 1, 3)]
-    arrive(ag_in)
-    for k in range(4):
-        outs.append(
-            pltpu.make_async_copy(ag.at[k], outb_ref.at[:, pl.ds(k * SPT, SPT)], l_out.at[5 + k])
-        )
+
+    def put(k, q):
+        lanes = pl.ds(pl.multiple_of(k * SPT, SPT), SPT)
+        outs.append(pltpu.make_async_copy(ag.at[k], outb_ref.at[:, lanes], l_out.at[5 + q]))
         outs[-1].start()
+
+    put(x, 0)
+    for dx, one in reversed(list(zip((2, 1, 3), ag_in))):
+        one.wait_recv()
+        put((x - dx) & 3, dx)
     for one in sends:
         one.wait_send()
 

time: 68.8 us -> 68.1 us (0.990)
  Pallas kernels: 68 us -> 67.3 us
where the time goes in v3:
time: 68.1 us; the launch traced here: 68 us
  Pallas kernels  67.3 us (99%)
    pallas_call x1, Pallas kernels, on_device(): pl.pallas_call(kernel, out_shape=shapes, in_specs=[hbm] * 4, out_specs=(h...  65.7 us
    pallas_call x1, Pallas kernels, on_device(): pl.pallas_call(settle, out_shape=shapes, in_specs=[vmem] * 3, out_specs=(...  1.59 us

profile of v3, /device:TPU:24, one launch (start us, length us, event | category | flops | bytes accessed | tf_op | source)
XLA Modules:
  0.0 68.0 jit_solution(951897030477009082)
XLA Ops:
  0.6 65.7 %sinkhorn.1 = (f32[1,512]{1,0:T(1,128)}, f32[1,8192]{1,0:T(1,128)}, f32[50,512]{1,0:T(8,128)}) custom-call(f32[50,512]{1,0:T(8,128)} %cells_ref.1, f32[50,128]{1,0:T(8,128)} %spots_ref.1, f32[1,512]{1,0:T(1,128)} %bitcast.6, f32[1,8192]{1,0:T(1,128)} %bitcast.4), custom_call_target="tpu_custom_call" | custom-call | flops 10737418240 | bytes 1048576 | tf_op jit(solution)/shard_map/sinkhorn/pallas_call | solution.py:476
  66.4 1.6 %settle.1 = (f32[1,512]{1,0:T(1,128)}, f32[1,8192]{1,0:T(1,128)}, f32[50,512]{1,0:T(8,128)}) custom-call(f32[1,512]{1,0:T(1,128)} %get-tuple-element.9.f_ref, f32[1,8192]{1,0:T(1,128)} %get-tuple-element.10.g_ref, f32[50,512]{1,0:T(8,128)} %get-tuple-element.11.b_ref), custom_call_target="tpu_custom_call" | custom-call | tf_op jit(solution)/shard_map/settle/pallas_call | solution.py:527

commit v4 on v3

--- a/solution.py
+++ b/solution.py
@@ -184,6 +184,9 @@
     near[3, 1].wait_recv()
     ref = cg.at[above, 1]
     far1 = start(ref, ref, s_half.at[1], r_half.at[1], (0, 3, 0, 0))
+    got(1)
+    got(2)
+    stream([slot_of(1, False), slot_of(2, False)], (0,))
     prep_cells(below, 0)
     prep_cells(above, 1)
     near[1, 1].wait_recv()
@@ -191,10 +194,7 @@
     near[3, 0].wait_recv()
     prep_cells(above, 0)
 
-    got(1)
-    got(2)
-    stream([slot_of(1, False), slot_of(2, False)], (0, 1, 3))
-    stream([s, z * 2 + 1 - c], (1, 3), False)
+    stream([s, z * 2 + 1 - c, slot_of(1, False), slot_of(2, False)], (1, 3), False)
 
     def four(k, carry):
         got(2 * k + 1)

time: 68.1 us -> 67.8 us (level)
  no operation moved by 1% of the time
where the time goes in v4:
time: 67.8 us; the launch traced here: 67.7 us
  Pallas kernels  67 us (99%)
    pallas_call x1, Pallas kernels, on_device(): pl.pallas_call(kernel, out_shape=shapes, in_specs=[hbm] * 4, out_specs=(h...  65.5 us
    pallas_call x1, Pallas kernels, on_device(): pl.pallas_call(settle, out_shape=shapes, in_specs=[vmem] * 3, out_specs=(...  1.59 us

profile of v4, /device:TPU:24, one launch (start us, length us, event | category | flops | bytes accessed | tf_op | source)
XLA Modules:
  0.0 67.7 jit_solution(5327965951584928877)
XLA Ops:
  0.6 65.5 %sinkhorn.1 = (f32[1,512]{1,0:T(1,128)}, f32[1,8192]{1,0:T(1,128)}, f32[50,512]{1,0:T(8,128)}) custom-call(f32[50,512]{1,0:T(8,128)} %cells_ref.1, f32[50,128]{1,0:T(8,128)} %spots_ref.1, f32[1,512]{1,0:T(1,128)} %bitcast.6, f32[1,8192]{1,0:T(1,128)} %bitcast.4), custom_call_target="tpu_custom_call" | custom-call | flops 10737418240 | bytes 1048576 | tf_op jit(solution)/shard_map/sinkhorn/pallas_call | solution.py:476
  66.1 1.6 %settle.1 = (f32[1,512]{1,0:T(1,128)}, f32[1,8192]{1,0:T(1,128)}, f32[50,512]{1,0:T(8,128)}) custom-call(f32[1,512]{1,0:T(1,128)} %get-tuple-element.9.f_ref, f32[1,8192]{1,0:T(1,128)} %get-tuple-element.10.g_ref, f32[50,512]{1,0:T(8,128)} %get-tuple-element.11.b_ref), custom_call_target="tpu_custom_call" | custom-call | tf_op jit(solution)/shard_map/settle/pallas_call | solution.py:527

commit v5 on v4

--- a/solution.py
+++ b/solution.py
@@ -94,6 +94,11 @@
         one.start()
         sends.append(one)
         return one
+
+    def settled(count):
+        for one in sends[:count]:
+            one.wait_send()
+        del sends[:count]
 
     def arrive(copies):
         for one in copies:
@@ -227,6 +232,7 @@
     def row_exchange(buf, ssem, rsem):
         return [start(buf.at[xy], buf.at[xy], ssem.at[k], rsem.at[k], peer) for k, peer in enumerate(row_peers)]
 
+    before = len(sends)
     moving = row_exchange(rb1, s_row1, r_row1)
     for k in range(TILE // 256):
         at[k * 256 : (k + 1) * 256, :] = ab[:, k * 256 : (k + 1) * 256].T
@@ -234,6 +240,13 @@
         for r in range(TILE // 256):
             rows = slice(r * 256, (r + 1) * 256)
             e[h, rows, :] = jnp.dot(at[rows, :], bb[:, h * HALF : (h + 1) * HALF], preferred_element_type=F32)
+    def drain(p, carry):
+        ring_copy(p).wait_send()
+        hand_on(p).wait_send()
+        return carry
+
+    settled(before)
+    lax.fori_loop(1, 8, drain, 0)
     arrive(lab_in)
     for k in range(4):
         pot[1:2, k * BLK : (k + 1) * BLK] = lab[k] * LOG2E
@@ -288,7 +301,10 @@
     mine = col_pass(c)
     half.wait_recv()
     cz1[z] = lse(jnp.concatenate([mine, cr1[...]], axis=0), 0)
-    arrive(ring_exchange(cz1, s_col1, r_col1))
+    before = len(sends)
+    moving = ring_exchange(cz1, s_col1, r_col1)
+    settled(before)
+    arrive(moving)
     gh1[c] = lbb[:, half_lanes(c)] * LOG2E - lse(cz1[...], 0)[0]
     back = start(gh1.at[c], gh1.at[c], s_pair.at[1], r_pair.at[1], sibling)
 
@@ -324,7 +340,10 @@
     scales(1 - c)
     row_sums(1 - c, True)
     to_row()
-    arrive(row_exchange(rb2, s_row2, r_row2))
+    before = len(sends)
+    moving = row_exchange(rb2, s_row2, r_row2)
+    settled(before)
+    arrive(moving)
     ratio = jnp.exp2(pot[1:2, :]) / jnp.sum(rb2[...], axis=0)
     u1, u2, u3 = pieces3(ratio)
     urow[0:1, :] = u1
@@ -350,6 +369,7 @@
     mine = col_sums(c)
     half.wait_recv()
     cz2[z] = mine + cr2[...]
+    before = len(sends)
     moving = ring_exchange(cz2, s_col2, r_col2)
     fo[...] = (pot[2:3, :] + jnp.log2(ratio)) * UNSCALE
     out_f = pltpu.make_async_copy(fo.at[:, pl.ds(pl.multiple_of(y * BLK, BLK), BLK)], outf_ref, l_out.at[0])
@@ -367,6 +387,7 @@
         return carry
 
     lax.fori_loop(0, TILE // RB, halve, 0)
+    settled(before)
     arrive(moving)
     gh2[c] = jnp.exp2(lbb[:, half_lanes(c)] * LOG2E) / jnp.sum(cz2[...], axis=0)
     back = start(gh2.at[c], gh2.at[c], s_pair.at[3], r_pair.at[3], sibling)
@@ -427,6 +448,7 @@
     whole = (xsum[0] + rs[4]) + (rs[8] + rs[12])
     ag[x] = whole[0:PC] / whole[PC : PC + 1, :]
     mine = ag.at[x]
+    before = len(sends)
     ag_in = [start(mine, mine, s_ag.at[dx], r_ag.at[dx], (dx, 0, 0, 0)) for dx in (2, 1, 3)]
     arrive(g_in)
     outs = [
@@ -441,18 +463,11 @@
         outs[-1].start()
 
     put(x, 0)
+    settled(before)
     for dx, one in reversed(list(zip((2, 1, 3), ag_in))):
         one.wait_recv()
         put((x - dx) & 3, dx)
-    for one in sends:
-        one.wait_send()
-
-    def drain(p, carry):
-        ring_copy(p).wait_send()
-        hand_on(p).wait_send()
-        return carry
-
-    lax.fori_loop(1, 8, drain, 0)
+    settled(len(sends))
     for one in [out_f] + outs:
         one.wait()
 

time: 67.8 us -> 67.8 us (level)
  no operation moved by 1% of the time
where the time goes in v5:
time: 67.8 us; the launch traced here: 67.7 us
  Pallas kernels  67 us (99%)
    pallas_call x1, Pallas kernels, on_device(): pl.pallas_call(kernel, out_shape=shapes, in_specs=[hbm] * 4, out_specs=(h...  65.5 us
    pallas_call x1, Pallas kernels, on_device(): pl.pallas_call(settle, out_shape=shapes, in_specs=[vmem] * 3, out_specs=(...  1.59 us

profile of v5, /device:TPU:24, one launch (start us, length us, event | category | flops | bytes accessed | tf_op | source)
XLA Modules:
  0.0 67.7 jit_solution(17950260034046277330)
XLA Ops:
  0.6 65.5 %sinkhorn.1 = (f32[1,512]{1,0:T(1,128)}, f32[1,8192]{1,0:T(1,128)}, f32[50,512]{1,0:T(8,128)}) custom-call(f32[50,512]{1,0:T(8,128)} %cells_ref.1, f32[50,128]{1,0:T(8,128)} %spots_ref.1, f32[1,512]{1,0:T(1,128)} %bitcast.6, f32[1,8192]{1,0:T(1,128)} %bitcast.4), custom_call_target="tpu_custom_call" | custom-call | flops 10737418240 | bytes 1048576 | tf_op jit(solution)/shard_map/sinkhorn/pallas_call | solution.py:491
  66.1 1.6 %settle.1 = (f32[1,512]{1,0:T(1,128)}, f32[1,8192]{1,0:T(1,128)}, f32[50,512]{1,0:T(8,128)}) custom-call(f32[1,512]{1,0:T(1,128)} %get-tuple-element.9.f_ref, f32[1,8192]{1,0:T(1,128)} %get-tuple-element.10.g_ref, f32[50,512]{1,0:T(8,128)} %get-tuple-element.11.b_ref), custom_call_target="tpu_custom_call" | custom-call | tf_op jit(solution)/shard_map/settle/pallas_call | solution.py:542

commit v6 on v4

--- a/solution.py
+++ b/solution.py
@@ -100,10 +100,9 @@
             one.wait_recv()
 
     near = {}
-    for dy in (1, 3):
-        for h in (0, 1) if dy == 1 else (1, 0):
-            ref = cg.at[y, h]
-            near[dy, h] = start(ref, ref, s_cell.at[dy, h], r_cell.at[dy, h], (0, dy, 0, 0))
+    for dy, h in ((1, 0), (3, 1), (1, 1), (3, 0)):
+        ref = cg.at[y, h]
+        near[dy, h] = start(ref, ref, s_cell.at[dy, h], r_cell.at[dy, h], (0, dy, 0, 0))
 
     def turn(p):
         return jnp.where((p & 1) == 1, (p + 1) // 2, 8 - p // 2)
@@ -175,8 +174,6 @@
     prep_cells(y, 0)
     prep_cells(y, 1)
     stream([s], (0,))
-    pair0.wait_recv()
-    stream([z * 2 + 1 - c], (0,))
     below, above = (y + 3) & 3, (y + 1) & 3
     near[1, 0].wait_recv()
     ref = cg.at[below, 0]
@@ -184,9 +181,10 @@
     near[3, 1].wait_recv()
     ref = cg.at[above, 1]
     far1 = start(ref, ref, s_half.at[1], r_half.at[1], (0, 3, 0, 0))
+    pair0.wait_recv()
     got(1)
     got(2)
-    stream([slot_of(1, False), slot_of(2, False)], (0,))
+    stream([z * 2 + 1 - c, slot_of(1, False), slot_of(2, False)], (0,))
     prep_cells(below, 0)
     prep_cells(above, 1)
     near[1, 1].wait_recv()

time: 67.8 us -> 67.8 us (level)
  no operation moved by 1% of the time
where the time goes in v6:
time: 67.8 us; the launch traced here: 67.7 us
  Pallas kernels  67 us (99%)
    pallas_call x1, Pallas kernels, on_device(): pl.pallas_call(kernel, out_shape=shapes, in_specs=[hbm] * 4, out_specs=(h...  65.4 us
    pallas_call x1, Pallas kernels, on_device(): pl.pallas_call(settle, out_shape=shapes, in_specs=[vmem] * 3, out_specs=(...  1.59 us

profile of v6, /device:TPU:24, one launch (start us, length us, event | category | flops | bytes accessed | tf_op | source)
XLA Modules:
  0.0 67.7 jit_solution(15419839532531768417)
XLA Ops:
  0.6 65.4 %sinkhorn.1 = (f32[1,512]{1,0:T(1,128)}, f32[1,8192]{1,0:T(1,128)}, f32[50,512]{1,0:T(8,128)}) custom-call(f32[50,512]{1,0:T(8,128)} %cells_ref.1, f32[50,128]{1,0:T(8,128)} %spots_ref.1, f32[1,512]{1,0:T(1,128)} %bitcast.6, f32[1,8192]{1,0:T(1,128)} %bitcast.4), custom_call_target="tpu_custom_call" | custom-call | flops 10737418240 | bytes 1048576 | tf_op jit(solution)/shard_map/sinkhorn/pallas_call | solution.py:474
  66.1 1.6 %settle.1 = (f32[1,512]{1,0:T(1,128)}, f32[1,8192]{1,0:T(1,128)}, f32[50,512]{1,0:T(8,128)}) custom-call(f32[1,512]{1,0:T(1,128)} %get-tuple-element.9.f_ref, f32[1,8192]{1,0:T(1,128)} %get-tuple-element.10.g_ref, f32[50,512]{1,0:T(8,128)} %get-tuple-element.11.b_ref), custom_call_target="tpu_custom_call" | custom-call | tf_op jit(solution)/shard_map/settle/pallas_call | solution.py:525
